TPU v7x, 32 devices: a whole 2x2x4 slice. The times are simulated.
32 devices in a mesh: groups: 2 (over y), expert: 16 (over z, x, core), sub: 1.
Axes of the slice: x: 2, y: 2, z: 4, core: 2. Of those that a mesh axis runs over, the one named last changes fastest.
Arguments:
- hidden: bfloat16 [4, 512, 8, 1024], P(None, ('groups', 'expert'), None, 'sub'), parts along dimension 1, may hold values from -6 to 6
- down_weight: bfloat16 [16, 1024, 3584], P('expert', None, 'sub'), may hold values from -0.1875 to 0.1875
- logits: float32 [4, 512, 8], P(None, ('groups', 'expert')), parts along dimension 1, may hold values from -6 to 6
- routes: int32 [4, 512, 8], P(None, ('groups', 'expert')), parts along dimension 1, may hold values from 0 to 15, all different within a row; in each aligned block of 16 rows (0 to 15, 16 to 31, ..., all dimensions but the last counted through in order) at most 16 rows name the same one
- placement: int32 [16], replicated, may hold values from 0 to 15, each once
- pair_slice: int32 [8, 16], P('groups', 'expert'), parts along dimension 0, may hold values from 0 to 31
Outputs:
- mixed: bfloat16 [4, 512, 3584], P(None, ('groups', 'expert'), 'sub'), parts along dimension 1
- swapped: bfloat16 [8, 16, 32, 3584], P('groups', 'expert', None, 'sub'), parts along dimension 0
There are 2 independent parts, one for each index of `groups`. A program takes and returns all parts, laid end to end along the dimension named above; an argument that names none is the same for every part. Nothing has to cross between parts.
Inputs may be any that keep to these rules, and one draw needn't show every extreme that they name: `routes`: each row names 8 different experts. In every aligned block of 16 rows (the tokens of one index of the expert axis in one step) no expert is named by more than 16 rows, a bound that some block reaches. `placement`: A permutation of the experts.
All inputs are finite; a program needn't handle non-finite values.
Results may differ from a plain program's by a relative error of at most 0.0049.
Values may be sent and summed in bfloat16 or wider, within the bound.
A program may use at most 64 MiB of HBM per device.

v0:
```python
import jax
import jax.numpy as jnp
from jax import lax
from jax.sharding import PartitionSpec as P

NSLICE = 32


ROUTE_SCALE = 2.5


def swapped(value, axis, stride):
    mask = 2**stride
    pairs = [(source, source ^ mask) for source in range(lax.axis_size(axis))]
    return lax.ppermute(value, axis, pairs)


def widen_rows(flat_rows):
    return lax.all_gather(flat_rows, "sub", axis=1, tiled=True)


def send_back(results):
    return lax.all_to_all(results, "expert", split_axis=0, concat_axis=0, tiled=True)


def per_device(hidden, down_weight, logits, routes, placement, pair_slice):
    steps, tok_rows, top_count, hidden_cols = hidden.shape
    devices = lax.axis_size("expert")
    capacity = min(tok_rows, 2 * ((tok_rows * top_count + devices - 1) // devices))
    weights = down_weight[0]
    slice_rows = weights.shape[0] // NSLICE
    expert_ids = jnp.arange(devices, dtype=jnp.int32)
    owners = jnp.sum(jnp.where(routes[..., None] == expert_ids, placement, 0), axis=-1)
    owners = owners.reshape(steps, tok_rows * top_count)
    onehot = (owners[..., None] == expert_ids).astype(jnp.int32)
    earlier = jnp.cumsum(onehot, axis=1) - onehot
    slot_of = jnp.sum(earlier * onehot, axis=2)
    slot_ids = jnp.arange(capacity, dtype=jnp.int32)
    chosen = ((onehot[..., None] == 1) & (slot_of[:, :, None, None] == slot_ids)).astype(
        jnp.bfloat16
    )
    chosen = chosen.reshape(steps, tok_rows * top_count, devices * capacity)
    scores = jax.nn.sigmoid(logits)
    gating = ROUTE_SCALE * scores / jnp.sum(scores, axis=-1, keepdims=True)
    token_rows = widen_rows(hidden.reshape(-1, hidden_cols)).reshape(
        steps, tok_rows * top_count, -1
    )
    levels = devices.bit_length() - 1
    mixed_all = []
    swapped_all = []
    for step in range(steps):
        outgoing = jnp.einsum(
            "qm,qw->mw", chosen[step], token_rows[step], preferred_element_type=jnp.float32
        )
        outgoing = outgoing.astype(jnp.bfloat16).reshape(devices, capacity, -1)
        received = lax.all_to_all(outgoing, "expert", split_axis=0, concat_axis=0, tiled=True)
        source_count, slot_count, columns = received.shape
        flat_rows = received.reshape(source_count * slot_count, columns)
        results = jnp.dot(flat_rows, weights, preferred_element_type=jnp.float32).astype(
            jnp.bfloat16
        )
        returned = send_back(results.reshape(source_count, slot_count, -1))
        per_slot = jnp.dot(
            chosen[step],
            returned.reshape(devices * capacity, -1),
            preferred_element_type=jnp.float32,
        )
        weighted = gating[step][..., None] * per_slot.reshape(tok_rows, top_count, -1)
        mixed_all.append(jnp.sum(weighted, axis=1).astype(jnp.bfloat16))
        swap_bit = levels - 1 - step % levels
        start_row = pair_slice[step, 0] * slice_rows
        own_slice = lax.dynamic_slice_in_dim(weights, start_row, slice_rows, 0)
        traded = swapped(own_slice, "expert", swap_bit)
        swapped_all.append(traded[None])
    return (jnp.stack(mixed_all), jnp.stack(swapped_all))


def solution(mesh):
    placed = (
        P(None, ("groups", "expert"), None, "sub"),
        P("expert", None, "sub"),
        P(None, ("groups", "expert"), None),
        P(None, ("groups", "expert"), None),
        P(),
        P("groups", "expert"),
    )
    return jax.shard_map(
        per_device,
        mesh=mesh,
        in_specs=placed,
        out_specs=(P(None, ("groups", "expert"), "sub"), P("groups", "expert", None, "sub")),
        check_vma=False,
    )
```

profile of v0, /device:TPU:0, one launch (start us, length us, event | category | flops | bytes accessed | tf_op | source)
XLA Modules:
  0.0 291.4 jit_solution(13636699730796375586)
XLA Ops:
  5.5 7.4 %all-to-all-start.6 = ((bf16[16,16,1024]{2,1,0:T(8,128)(2,1)}), bf16[16,16,1024]{2,1,0:T(8,128)(2,1)S(1)}, u32[]{:S(2)}, u32[]{:S(2)}) async-start(bf16[16,16,1024]{2,1,0:T(8,128)(2,1)} %bitcast.31), calls=%async_computation.6 | async-start | bytes 1048576 | tf_op jit(solution)/shard_map/all_to_all | solution.py:56
  14.0 13.4 %all-to-all-done.6 = bf16[16,16,1024]{2,1,0:T(8,128)(2,1)S(1)} async-done(((bf16[16,16,1024]{2,1,0:T(8,128)(2,1)}), bf16[16,16,1024]{2,1,0:T(8,128)(2,1)S(1)}, u32[]{:S(2)}, u32[]{:S(2)}) %all-to-all-start.6) | async-done | bytes 524320 | tf_op jit(solution)/shard_map/all_to_all | solution.py:56
  27.3 4.1 %all-to-all-start.4 = ((bf16[16,16,1024]{2,1,0:T(8,128)(2,1)}), bf16[16,16,1024]{2,1,0:T(8,128)(2,1)S(1)}, u32[]{:S(2)}, u32[]{:S(2)}) async-start(bf16[16,16,1024]{2,1,0:T(8,128)(2,1)} %bitcast.22), calls=%async_computation.4 | async-start | bytes 1048576 | tf_op jit(solution)/shard_map/all_to_all | solution.py:56
  32.5 13.4 %all-to-all-done.4 = bf16[16,16,1024]{2,1,0:T(8,128)(2,1)S(1)} async-done(((bf16[16,16,1024]{2,1,0:T(8,128)(2,1)}), bf16[16,16,1024]{2,1,0:T(8,128)(2,1)S(1)}, u32[]{:S(2)}, u32[]{:S(2)}) %all-to-all-start.4) | async-done | bytes 524320 | tf_op jit(solution)/shard_map/all_to_all | solution.py:56
  45.9 4.1 %all-to-all-start.2 = ((bf16[16,16,1024]{2,1,0:T(8,128)(2,1)}), bf16[16,16,1024]{2,1,0:T(8,128)(2,1)S(1)}, u32[]{:S(2)}, u32[]{:S(2)}) async-start(bf16[16,16,1024]{2,1,0:T(8,128)(2,1)} %bitcast.13), calls=%async_computation.2 | async-start | bytes 1048576 | tf_op jit(solution)/shard_map/all_to_all | solution.py:56
  51.1 13.4 %all-to-all-done.2 = bf16[16,16,1024]{2,1,0:T(8,128)(2,1)S(1)} async-done(((bf16[16,16,1024]{2,1,0:T(8,128)(2,1)}), bf16[16,16,1024]{2,1,0:T(8,128)(2,1)S(1)}, u32[]{:S(2)}, u32[]{:S(2)}) %all-to-all-start.2) | async-done | bytes 524320 | tf_op jit(solution)/shard_map/all_to_all | solution.py:56
  64.5 4.1 %all-to-all-start = ((bf16[16,16,1024]{2,1,0:T(8,128)(2,1)}), bf16[16,16,1024]{2,1,0:T(8,128)(2,1)S(1)}, u32[]{:S(2)}, u32[]{:S(2)}) async-start(bf16[16,16,1024]{2,1,0:T(8,128)(2,1)} %bitcast.3), calls=%async_computation | async-start | bytes 1048576 | tf_op jit(solution)/shard_map/all_to_all | solution.py:56
  68.6 6.4 %fusion.17 = bf16[256,3584]{1,0:T(8,128)(2,1)} fusion(bf16[256,1024]{1,0:T(8,128)(2,1)S(1)} %bitcast.125, bf16[1,1024,3584]{2,1,0:T(8,128)(2,1)} %param.7), kind=kOutput, calls=%fused_computation.11 | convolution fusion | flops 1879965696 | bytes 9699328 | tf_op jit(solution)/shard_map/dot_general | solution.py:59
  75.0 8.0 %all-to-all-done = bf16[16,16,1024]{2,1,0:T(8,128)(2,1)S(1)} async-done(((bf16[16,16,1024]{2,1,0:T(8,128)(2,1)}), bf16[16,16,1024]{2,1,0:T(8,128)(2,1)S(1)}, u32[]{:S(2)}, u32[]{:S(2)}) %all-to-all-start) | async-done | bytes 524320 | tf_op jit(solution)/shard_map/all_to_all | solution.py:56
  83.1 4.1 %all-to-all-start.7 = ((bf16[16,16,3584]{2,1,0:T(8,128)(2,1)}), bf16[16,16,3584]{2,1,0:T(8,128)(2,1)S(1)}, u32[]{:S(2)}, u32[]{:S(2)}) async-start(bf16[16,16,3584]{2,1,0:T(8,128)(2,1)} %bitcast.119), calls=%async_computation.7 | async-start | bytes 3670016 | tf_op jit(solution)/shard_map/all_to_all | solution.py:23
  87.2 6.4 %fusion.14 = bf16[256,3584]{1,0:T(8,128)(2,1)} fusion(bf16[256,1024]{1,0:T(8,128)(2,1)S(1)} %bitcast.124, bf16[1,1024,3584]{2,1,0:T(8,128)(2,1)} %param.7), kind=kOutput, calls=%fused_computation.10 | convolution fusion | flops 1879965696 | bytes 9699328 | tf_op jit(solution)/shard_map/dot_general | solution.py:59
  93.6 30.1 %all-to-all-done.7 = bf16[16,16,3584]{2,1,0:T(8,128)(2,1)S(1)} async-done(((bf16[16,16,3584]{2,1,0:T(8,128)(2,1)}), bf16[16,16,3584]{2,1,0:T(8,128)(2,1)S(1)}, u32[]{:S(2)}, u32[]{:S(2)}) %all-to-all-start.7) | async-done | bytes 1835040 | tf_op jit(solution)/shard_map/all_to_all | solution.py:23
  123.7 10.2 %all-to-all-start.5 = ((bf16[16,16,3584]{2,1,0:T(8,128)(2,1)}), bf16[16,16,3584]{2,1,0:T(8,128)(2,1)}, u32[]{:S(2)}, u32[]{:S(2)}) async-start(bf16[16,16,3584]{2,1,0:T(8,128)(2,1)} %bitcast.120), calls=%async_computation.5 | async-start | bytes 3670016 | tf_op jit(solution)/shard_map/all_to_all | solution.py:23
  133.9 6.4 %fusion.11 = bf16[256,3584]{1,0:T(8,128)(2,1)} fusion(bf16[256,1024]{1,0:T(8,128)(2,1)S(1)} %bitcast.122, bf16[1,1024,3584]{2,1,0:T(8,128)(2,1)} %param.7), kind=kOutput, calls=%fused_computation.9 | convolution fusion | flops 1879965696 | bytes 9699328 | tf_op jit(solution)/shard_map/dot_general | solution.py:59
  140.4 30.2 %all-to-all-done.5 = bf16[16,16,3584]{2,1,0:T(8,128)(2,1)} async-done(((bf16[16,16,3584]{2,1,0:T(8,128)(2,1)}), bf16[16,16,3584]{2,1,0:T(8,128)(2,1)}, u32[]{:S(2)}, u32[]{:S(2)}) %all-to-all-start.5) | async-done | bytes 1835040 | tf_op jit(solution)/shard_map/all_to_all | solution.py:23
  170.5 10.2 %all-to-all-start.3 = ((bf16[16,16,3584]{2,1,0:T(8,128)(2,1)}), bf16[16,16,3584]{2,1,0:T(8,128)(2,1)}, u32[]{:S(2)}, u32[]{:S(2)}) async-start(bf16[16,16,3584]{2,1,0:T(8,128)(2,1)} %bitcast.121), calls=%async_computation.3 | async-start | bytes 3670016 | tf_op jit(solution)/shard_map/all_to_all | solution.py:23
  180.7 6.4 %fusion.8 = bf16[256,3584]{1,0:T(8,128)(2,1)} fusion(bf16[256,1024]{1,0:T(8,128)(2,1)S(1)} %bitcast.123, bf16[1,1024,3584]{2,1,0:T(8,128)(2,1)} %param.7), kind=kOutput, calls=%fused_computation.8 | convolution fusion | flops 1879965696 | bytes 9699328 | tf_op jit(solution)/shard_map/dot_general | solution.py:59
  187.1 30.2 %all-to-all-done.3 = bf16[16,16,3584]{2,1,0:T(8,128)(2,1)} async-done(((bf16[16,16,3584]{2,1,0:T(8,128)(2,1)}), bf16[16,16,3584]{2,1,0:T(8,128)(2,1)}, u32[]{:S(2)}, u32[]{:S(2)}) %all-to-all-start.3) | async-done | bytes 1835040 | tf_op jit(solution)/shard_map/all_to_all | solution.py:23
  217.3 10.3 %all-to-all-start.1 = ((bf16[16,16,3584]{2,1,0:T(8,128)(2,1)}), bf16[16,16,3584]{2,1,0:T(8,128)(2,1)}, u32[]{:S(2)}, u32[]{:S(2)}) async-start(bf16[16,16,3584]{2,1,0:T(8,128)(2,1)} %bitcast.118), calls=%async_computation.1 | async-start | bytes 3670016 | tf_op jit(solution)/shard_map/all_to_all | solution.py:23
  236.6 2.4 collective-permute-start
  243.6 6.4 %collective-permute-done.2 = bf16[32,3584]{1,0:T(8,128)(2,1)S(1)} collective-permute-done((bf16[32,3584]{1,0:T(8,128)(2,1)}, bf16[32,3584]{1,0:T(8,128)(2,1)S(1)}, u32[]{:S(2)}, u32[]{:S(2)}) %collective-permute-start.2) | collective-permute-done | bytes 229408 | tf_op jit(solution)/shard_map/ppermute | solution.py:15
  250.0 13.6 %collective-permute-done.1 = bf16[32,3584]{1,0:T(8,128)(2,1)} collective-permute-done((bf16[32,3584]{1,0:T(8,128)(2,1)}, bf16[32,3584]{1,0:T(8,128)(2,1)}, u32[]{:S(2)}, u32[]{:S(2)}) %collective-permute-start.1) | collective-permute-done | bytes 229408 | tf_op jit(solution)/shard_map/ppermute | solution.py:15
  263.6 17.4 %collective-permute-done = bf16[32,3584]{1,0:T(8,128)(2,1)} collective-permute-done((bf16[32,3584]{1,0:T(8,128)(2,1)}, bf16[32,3584]{1,0:T(8,128)(2,1)}, u32[]{:S(2)}, u32[]{:S(2)}) %collective-permute-start) | collective-permute-done | bytes 229408 | tf_op jit(solution)/shard_map/ppermute | solution.py:15
  283.8 2.2 fusion.22
  (47 shorter events, 27.1 us)
Async XLA Ops:
  0.6 3.8 %copy-start = (bf16[4,16,8,1024]{3,2,1,0:T(8,128)(2,1)S(1)}, bf16[4,16,8,1024]{3,2,1,0:T(8,128)(2,1)}, u32[]{:S(2)}) copy-start(bf16[4,16,8,1024]{3,2,1,0:T(8,128)(2,1)} %param.6) | copy-start | bytes 3145732
  5.5 21.8 %all-to-all-start.6 = ((bf16[16,16,1024]{2,1,0:T(8,128)(2,1)}), bf16[16,16,1024]{2,1,0:T(8,128)(2,1)S(1)}, u32[]{:S(2)}, u32[]{:S(2)}) async-start(bf16[16,16,1024]{2,1,0:T(8,128)(2,1)} %bitcast.31), calls=%async_computation.6 | async-start | bytes 1048576 | tf_op jit(solution)/shard_map/all_to_all | solution.py:56
  27.3 18.6 %all-to-all-start.4 = ((bf16[16,16,1024]{2,1,0:T(8,128)(2,1)}), bf16[16,16,1024]{2,1,0:T(8,128)(2,1)S(1)}, u32[]{:S(2)}, u32[]{:S(2)}) async-start(bf16[16,16,1024]{2,1,0:T(8,128)(2,1)} %bitcast.22), calls=%async_computation.4 | async-start | bytes 1048576 | tf_op jit(solution)/shard_map/all_to_all | solution.py:56
  45.9 18.6 %all-to-all-start.2 = ((bf16[16,16,1024]{2,1,0:T(8,128)(2,1)}), bf16[16,16,1024]{2,1,0:T(8,128)(2,1)S(1)}, u32[]{:S(2)}, u32[]{:S(2)}) async-start(bf16[16,16,1024]{2,1,0:T(8,128)(2,1)} %bitcast.13), calls=%async_computation.2 | async-start | bytes 1048576 | tf_op jit(solution)/shard_map/all_to_all | solution.py:56
  64.5 18.6 %all-to-all-start = ((bf16[16,16,1024]{2,1,0:T(8,128)(2,1)}), bf16[16,16,1024]{2,1,0:T(8,128)(2,1)S(1)}, u32[]{:S(2)}, u32[]{:S(2)}) async-start(bf16[16,16,1024]{2,1,0:T(8,128)(2,1)} %bitcast.3), calls=%async_computation | async-start | bytes 1048576 | tf_op jit(solution)/shard_map/all_to_all | solution.py:56
  83.1 40.6 %all-to-all-start.7 = ((bf16[16,16,3584]{2,1,0:T(8,128)(2,1)}), bf16[16,16,3584]{2,1,0:T(8,128)(2,1)S(1)}, u32[]{:S(2)}, u32[]{:S(2)}) async-start(bf16[16,16,3584]{2,1,0:T(8,128)(2,1)} %bitcast.119), calls=%async_computation.7 | async-start | bytes 3670016 | tf_op jit(solution)/shard_map/all_to_all | solution.py:23
  123.7 46.8 %all-to-all-start.5 = ((bf16[16,16,3584]{2,1,0:T(8,128)(2,1)}), bf16[16,16,3584]{2,1,0:T(8,128)(2,1)}, u32[]{:S(2)}, u32[]{:S(2)}) async-start(bf16[16,16,3584]{2,1,0:T(8,128)(2,1)} %bitcast.120), calls=%async_computation.5 | async-start | bytes 3670016 | tf_op jit(solution)/shard_map/all_to_all | solution.py:23
  170.5 46.8 %all-to-all-start.3 = ((bf16[16,16,3584]{2,1,0:T(8,128)(2,1)}), bf16[16,16,3584]{2,1,0:T(8,128)(2,1)}, u32[]{:S(2)}, u32[]{:S(2)}) async-start(bf16[16,16,3584]{2,1,0:T(8,128)(2,1)} %bitcast.121), calls=%async_computation.3 | async-start | bytes 3670016 | tf_op jit(solution)/shard_map/all_to_all | solution.py:23
  217.3 10.4 %copy-start.2 = (s32[4,1]{0,1:T(1,128)S(1)}, s32[4,1]{0,1:T(1,128)}, u32[]{:S(2)}) copy-start(s32[4,1]{0,1:T(1,128)} %param.11) | copy-start | bytes 52
  217.3 71.0 %all-to-all-start.1 = ((bf16[16,16,3584]{2,1,0:T(8,128)(2,1)}), bf16[16,16,3584]{2,1,0:T(8,128)(2,1)}, u32[]{:S(2)}, u32[]{:S(2)}) async-start(bf16[16,16,3584]{2,1,0:T(8,128)(2,1)} %bitcast.118), calls=%async_computation.1 | async-start | bytes 3670016 | tf_op jit(solution)/shard_map/all_to_all | solution.py:23
  227.7 11.3 %copy-start.1 = (f32[4,16,8]{1,2,0:T(8,128)S(1)}, f32[4,16,8]{1,2,0:T(8,128)}, u32[]{:S(2)}) copy-start(f32[4,16,8]{1,2,0:T(8,128)} %param.8) | copy-start | bytes 6148
  233.1 10.4 %collective-permute-start.3 = (bf16[32,3584]{1,0:T(8,128)(2,1)}, bf16[32,3584]{1,0:T(8,128)(2,1)S(1)}, u32[]{:S(2)}, u32[]{:S(2)}) collective-permute-start(bf16[32,3584]{1,0:T(8,128)(2,1)} %get-tuple-element.4), channel_id=1, source_target_pairs={{0,1},{1,0},{2,3},{3,2},{4,5},{5,4},{6,7},{7,6},{8,9},{9,8},{10,11... | collective-permute-start | bytes 688136 | tf_op jit(solution)/shard_map/ppermute | solution.py:15
  233.5 16.5 %collective-permute-start.2 = (bf16[32,3584]{1,0:T(8,128)(2,1)}, bf16[32,3584]{1,0:T(8,128)(2,1)S(1)}, u32[]{:S(2)}, u32[]{:S(2)}) collective-permute-start(bf16[32,3584]{1,0:T(8,128)(2,1)} %get-tuple-element.5), channel_id=1, source_target_pairs={{0,2},{1,3},{2,0},{3,1},{4,6},{5,7},{6,4},{7,5},{8,10},{9,11},{10,... | collective-permute-start | bytes 688136 | tf_op jit(solution)/shard_map/ppermute | solution.py:15
  235.2 28.4 %collective-permute-start.1 = (bf16[32,3584]{1,0:T(8,128)(2,1)}, bf16[32,3584]{1,0:T(8,128)(2,1)}, u32[]{:S(2)}, u32[]{:S(2)}) collective-permute-start(bf16[32,3584]{1,0:T(8,128)(2,1)} %get-tuple-element.3), channel_id=1, source_target_pairs={{0,4},{1,5},{2,6},{3,7},{4,0},{5,1},{6,2},{7,3},{8,12},{9,13},{10,... | collective-permute-start | bytes 688136 | tf_op jit(solution)/shard_map/ppermute | solution.py:15
  236.6 44.4 %collective-permute-start = (bf16[32,3584]{1,0:T(8,128)(2,1)}, bf16[32,3584]{1,0:T(8,128)(2,1)}, u32[]{:S(2)}, u32[]{:S(2)}) collective-permute-start(bf16[32,3584]{1,0:T(8,128)(2,1)} %get-tuple-element.2), channel_id=1, source_target_pairs={{0,8},{1,9},{2,10},{3,11},{4,12},{5,13},{6,14},{7,15},{8,0},{9,1},... | collective-permute-start | bytes 688136 | tf_op jit(solution)/shard_map/ppermute | solution.py:15
where the time goes:
time: 292 us; the launch traced here: 291 us
  waiting for transfers between devices  176 us (60%)
  starting transfers between devices  60.4 us (21%)
  matrix products  37.4 us (13%)
  local copies, waits for them, and re-layouts  8.43 us (3%)
  other arithmetic  5.59 us (2%)
  between operations  3.44 us (1%)
    all_to_all x4, waiting for transfers between devices, send_back(): lax.all_to_all(results, 'expert', split_axis=0, concat_axis=0, tiled=True)  90.5 us
    all_to_all x4, waiting for transfers between devices, per_device(): lax.all_to_all(outgoing, 'expert', split_axis=0, concat_axis=0, tiled=True)  48.1 us
    ppermute x4, waiting for transfers between devices, swapped(): return lax.ppermute(value, axis, pairs)  37.4 us
    all_to_all x4, starting transfers between devices, send_back(): lax.all_to_all(results, 'expert', split_axis=0, concat_axis=0, tiled=True)  34.9 us
    dot_general x4, matrix products, per_device(): jnp.dot(flat_rows, weights, preferred_element_type=jnp.float32)  25.7 us
    all_to_all x4, starting transfers between devices, per_device(): lax.all_to_all(outgoing, 'expert', split_axis=0, concat_axis=0, tiled=True)  19.7 us
    dot_general x4, matrix products, per_device(): jnp.dot(chosen[step], returned.reshape(devices * capacity, -1), preferred...  7.39 us
    ppermute x4, starting transfers between devices, swapped(): return lax.ppermute(value, axis, pairs)  5.86 us
  transfers between devices with their start and end apart: 12, of which 10 were waited for; matrix products, arithmetic and copies ran while one was open for 15% of the time, Pallas kernels for 0%

commit v1 on v0

--- a/solution.py
+++ b/solution.py
@@ -1,9 +1,14 @@
+import functools
 import jax
 import jax.numpy as jnp
 from jax import lax
+from jax.experimental import pallas as pl
+from jax.experimental.pallas import tpu as pltpu
 from jax.sharding import PartitionSpec as P
 
+MESH = pl.DeviceIdType.MESH
 NSLICE = 32
+VMEM_BYTES = 60 * 2**20
 
 
 ROUTE_SCALE = 2.5
@@ -23,7 +28,7 @@
     return lax.all_to_all(results, "expert", split_axis=0, concat_axis=0, tiled=True)
 
 
-def per_device(hidden, down_weight, logits, routes, placement, pair_slice):
+def plain_device(hidden, down_weight, logits, routes, placement, pair_slice):
     steps, tok_rows, top_count, hidden_cols = hidden.shape
     devices = lax.axis_size("expert")
     capacity = min(tok_rows, 2 * ((tok_rows * top_count + devices - 1) // devices))
@@ -75,6 +80,301 @@
     return (jnp.stack(mixed_all), jnp.stack(swapped_all))
 
 
+def kernel(
+    n, hidden_hbm, weight_hbm, owners_ref, gating_ref, pair_ref, mixed_ref, swapped_ref,
+    hid, weights, outbox, inbox, acc, core_out, core_in, x_out, x_in,
+    up_out, up_in, down_out, down_in, swap_out,
+    local_sem, hid_send, hid_recv, core_sem, x_sem, up_sem, down_sem, swap_sem,
+):
+    steps = hid.shape[0]
+    rows = hid.shape[1]
+    tok = inbox.shape[2]
+    top = rows // tok
+    width = weights.shape[1]
+    tile = 512
+    planes = n // 4
+    me = lax.axis_index("expert")
+    c = lax.rem(me, 2)
+    x = lax.rem(me // 2, 2)
+    z = me // 4
+    core_mate = me + 1 - 2 * c
+    x_mate = me + 2 - 4 * x
+
+    def local(s):
+        return pltpu.make_async_copy(hidden_hbm.at[s], hid.at[s], local_sem.at[s])
+
+    weight_copy = pltpu.make_async_copy(weight_hbm, weights, local_sem.at[steps])
+    for s in range(steps):
+        local(s).start()
+    weight_copy.start()
+
+    barrier = pltpu.get_barrier_semaphore()
+
+    @pl.loop(1, n)
+    def _(j):
+        pl.semaphore_signal(
+            barrier, inc=1, device_id={"expert": lax.rem(me + j, n)}, device_id_type=MESH
+        )
+
+    pl.semaphore_wait(barrier, n - 1)
+
+    def remote(src, dst, send, recv, target):
+        return pltpu.make_async_remote_copy(
+            src_ref=src, dst_ref=dst, send_sem=send, recv_sem=recv,
+            device_id={"expert": target}, device_id_type=MESH,
+        )
+
+    def hidden_to(s, target):
+        return remote(
+            outbox.at[s, target], inbox.at[s, me], hid_send.at[s, target], hid_recv.at[s, me], target
+        )
+
+    def hidden_from(s, source):
+        return remote(
+            outbox.at[s, source], inbox.at[s, source], hid_send.at[s, source],
+            hid_recv.at[s, source], source,
+        )
+
+    slot = lax.broadcasted_iota(jnp.int32, (n * tok, rows), 0)
+    choice = lax.broadcasted_iota(jnp.int32, (n * tok, rows), 1)
+    same_token = lax.rem(slot, tok) == choice // top
+    target_of = slot // tok
+    for s in range(steps):
+        picked = same_token & (owners_ref[s] == target_of)
+        scale = jnp.sum(jnp.where(picked, gating_ref[s], 0.0), axis=1, keepdims=True)
+        chosen = jnp.where(picked, 1.0, 0.0).astype(jnp.bfloat16)
+        local(s).wait()
+        dense = jnp.dot(chosen, hid[s], preferred_element_type=jnp.float32) * scale
+        outbox[s] = dense.astype(jnp.bfloat16).reshape(n, tok, dense.shape[1])
+
+        @pl.loop(1, n)
+        def _(j):
+            hidden_to(s, lax.rem(me + j, n)).start()
+
+        inbox[s, me] = outbox[s, me]
+
+    weight_copy.wait()
+    levels = n.bit_length() - 1
+    slice_rows = swap_out.shape[1]
+    row = lax.broadcasted_iota(jnp.int32, (slice_rows, weights.shape[0]), 0)
+    unit = lax.broadcasted_iota(jnp.int32, (slice_rows, weights.shape[0]), 1)
+    handed = jnp.concatenate(
+        [jnp.where(unit == row + pair_ref[s, 0] * slice_rows, 1.0, 0.0) for s in range(steps)]
+    ).astype(jnp.bfloat16)
+
+    @pl.loop(0, width // tile)
+    def _(j):
+        columns = pl.ds(pl.multiple_of(j * tile, tile), tile)
+        block = jnp.dot(handed, weights[:, columns], preferred_element_type=jnp.float32)
+        swap_out[:, :, columns] = block.astype(jnp.bfloat16).reshape(steps, slice_rows, tile)
+
+    swaps = []
+    for s in range(steps):
+        stride = 2 ** (levels - 1 - s % levels)
+        partner = me + stride - 2 * stride * lax.rem(me // stride, 2)
+        swaps.append(
+            remote(swap_out.at[s], swapped_ref.at[s, 0], swap_sem.at[0, s], swap_sem.at[1, s], partner)
+        )
+
+    def core_copy(s):
+        return remote(core_out.at[s], core_in.at[s], core_sem.at[0, s], core_sem.at[1, s], core_mate)
+
+    def x_copy(s):
+        return remote(x_out.at[s], x_in.at[s], x_sem.at[0, s], x_sem.at[1, s], x_mate)
+
+    def up_copy(s, hop):
+        part = pl.ds(hop + 1, planes - 1 - hop)
+        return remote(
+            up_out.at[s, part], up_in.at[s, part], up_sem.at[0, s], up_sem.at[1, s], me + 4
+        )
+
+    def down_copy(s, hop):
+        part = pl.ds(0, planes - 1 - hop)
+        return remote(
+            down_out.at[s, part], down_in.at[s, part], down_sem.at[0, s], down_sem.at[1, s], me - 4
+        )
+
+    def product(s):
+        @pl.loop(1, n)
+        def _(j):
+            hidden_from(s, lax.rem(me + j, n)).wait_recv()
+
+        @pl.loop(0, width // tile)
+        def _(j):
+            columns = pl.ds(pl.multiple_of(j * tile, tile), tile)
+            block = jnp.dot(
+                inbox[s].reshape(n * tok, inbox.shape[3]), weights[:, columns],
+                preferred_element_type=jnp.float32,
+            )
+            acc[s, :, :, columns] = block.reshape(n, tok, tile)
+
+        @pl.loop(0, n // 2)
+        def _(q):
+            core_out[s, q] = acc[s, 2 * q + 1 - c].astype(jnp.bfloat16)
+
+        core_copy(s).start()
+
+    def across_x(s):
+        core_copy(s).wait_recv()
+
+        @pl.loop(0, planes)
+        def _(p):
+            q = 2 * p + 1 - x
+            x_out[s, p] = (acc[s, 2 * q + c] + core_in[s, q].astype(jnp.float32)).astype(jnp.bfloat16)
+
+        x_copy(s).start()
+
+    def plane_sum(s, p):
+        q = 2 * p + x
+        return (
+            acc[s, 2 * q + c] + core_in[s, q].astype(jnp.float32) + x_in[s, p].astype(jnp.float32)
+        )
+
+    def along_z(s, hop):
+        if hop == 0:
+            x_copy(s).wait_recv()
+
+        @pl.when(z == hop)
+        def _():
+            if hop:
+                up_copy(s, hop - 1).wait_recv()
+
+            @pl.loop(hop + 1, planes)
+            def _(p):
+                total = plane_sum(s, p)
+                if hop:
+                    total = total + up_in[s, p].astype(jnp.float32)
+                up_out[s, p] = total.astype(jnp.bfloat16)
+
+            up_copy(s, hop).start()
+
+        @pl.when(z == planes - 1 - hop)
+        def _():
+            if hop:
+                down_copy(s, hop - 1).wait_recv()
+
+            @pl.loop(0, planes - 1 - hop)
+            def _(p):
+                total = plane_sum(s, p)
+                if hop:
+                    total = total + down_in[s, p].astype(jnp.float32)
+                down_out[s, p] = total.astype(jnp.bfloat16)
+
+            down_copy(s, hop).start()
+
+    def finish(s):
+        @pl.when(z == planes - 1)
+        def _():
+            up_copy(s, planes - 2).wait_recv()
+            mixed_ref[s] = (plane_sum(s, z) + up_in[s, z].astype(jnp.float32)).astype(mixed_ref.dtype)
+
+        @pl.when(z == 0)
+        def _():
+            down_copy(s, planes - 2).wait_recv()
+            mixed_ref[s] = (plane_sum(s, z) + down_in[s, z].astype(jnp.float32)).astype(mixed_ref.dtype)
+
+        @pl.when((z > 0) & (z < planes - 1))
+        def _():
+            total = plane_sum(s, z) + up_in[s, z].astype(jnp.float32) + down_in[s, z].astype(jnp.float32)
+            mixed_ref[s] = total.astype(mixed_ref.dtype)
+
+    hops = planes - 1
+    for i in range(steps + hops + 1):
+        if i < steps:
+            product(i)
+            swaps[i].start()
+        for hop in range(hops - 1, 0, -1):
+            if 0 <= i - 1 - hop < steps:
+                along_z(i - 1 - hop, hop)
+        if i < steps:
+            across_x(i)
+        if 0 <= i - 1 < steps:
+            along_z(i - 1, 0)
+        if 0 <= i - 1 - hops < steps:
+            finish(i - 1 - hops)
+
+    for s in range(steps):
+        @pl.loop(1, n)
+        def _(j):
+            hidden_to(s, lax.rem(me + j, n)).wait_send()
+
+        swaps[s].wait()
+        core_copy(s).wait_send()
+        x_copy(s).wait_send()
+        for hop in range(hops):
+            @pl.when(z == hop)
+            def _():
+                up_copy(s, hop).wait_send()
+
+            @pl.when(z == planes - 1 - hop)
+            def _():
+                down_copy(s, hop).wait_send()
+
+
+def kernel_device(hidden, down_weight, logits, routes, placement, pair_slice):
+    steps, tok, top, hidden_cols = hidden.shape
+    n = lax.axis_size("expert")
+    weights = down_weight[0]
+    width = weights.shape[1]
+    slice_rows = weights.shape[0] // NSLICE
+    expert_ids = jnp.arange(n, dtype=jnp.int32)
+    owners = jnp.sum(jnp.where(routes[..., None] == expert_ids, placement, 0), axis=-1)
+    scores = jax.nn.sigmoid(logits)
+    gating = ROUTE_SCALE * scores / jnp.sum(scores, axis=-1, keepdims=True)
+    planes = n // 4
+    b16, f32 = jnp.bfloat16, jnp.float32
+    dma = pltpu.SemaphoreType.DMA
+    anywhere = pl.BlockSpec(memory_space=pl.ANY)
+    vmem = pl.BlockSpec(memory_space=pltpu.VMEM)
+    return pl.pallas_call(
+        functools.partial(kernel, n),
+        out_shape=(
+            jax.ShapeDtypeStruct((steps, tok, width), b16),
+            jax.ShapeDtypeStruct((steps, 1, slice_rows, width), b16),
+        ),
+        in_specs=[anywhere, anywhere, vmem, vmem, pl.BlockSpec(memory_space=pltpu.SMEM)],
+        out_specs=(vmem, anywhere),
+        scratch_shapes=[
+            pltpu.VMEM((steps, tok * top, hidden_cols), b16),
+            pltpu.VMEM(weights.shape, b16),
+            pltpu.VMEM((steps, n, tok, hidden_cols), b16),
+            pltpu.VMEM((steps, n, tok, hidden_cols), b16),
+            pltpu.VMEM((steps, n, tok, width), f32),
+            pltpu.VMEM((steps, n // 2, tok, width), b16),
+            pltpu.VMEM((steps, n // 2, tok, width), b16),
+            pltpu.VMEM((steps, planes, tok, width), b16),
+            pltpu.VMEM((steps, planes, tok, width), b16),
+            pltpu.VMEM((steps, planes, tok, width), b16),
+            pltpu.VMEM((steps, planes, tok, width), b16),
+            pltpu.VMEM((steps, planes, tok, width), b16),
+            pltpu.VMEM((steps, planes, tok, width), b16),
+            pltpu.VMEM((steps, slice_rows, width), b16),
+            dma((steps + 1,)), dma((steps, n)), dma((steps, n)), dma((2, steps)), dma((2, steps)),
+            dma((2, steps)), dma((2, steps)), dma((2, steps)),
+        ],
+        compiler_params=pltpu.CompilerParams(
+            collective_id=0, has_side_effects=True, vmem_limit_bytes=VMEM_BYTES
+        ),
+    )(
+        hidden.reshape(steps, tok * top, hidden_cols),
+        weights,
+        owners.reshape(steps, 1, tok * top),
+        gating.reshape(steps, 1, tok * top),
+        pair_slice,
+    )
+
+
+def per_device(hidden, down_weight, logits, routes, placement, pair_slice):
+    steps, tok, top, hidden_cols = hidden.shape
+    n = lax.axis_size("expert")
+    width = down_weight.shape[2]
+    capacity = min(tok, 2 * ((tok * top + n - 1) // n))
+    held = n * tok * width * steps * 11
+    fits = n % 8 == 0 and capacity == tok and lax.axis_size("sub") == 1 and held < VMEM_BYTES
+    body = kernel_device if fits and width % 512 == 0 else plain_device
+    return body(hidden, down_weight, logits, routes, placement, pair_slice)
+
+
 def solution(mesh):
     placed = (
         P(None, ("groups", "expert"), None, "sub"),

time: 292 us -> 119 us (0.41)
  waiting for transfers between devices: 176 us -> 0 us
  Pallas kernels: 0 us -> 107 us
  starting transfers between devices: 60.4 us -> 0 us
  matrix products: 37.4 us -> 0 us
    all_to_all x8 -> x0, waiting for transfers between devices: 139 us -> none  [the longest x4 90.5 us: send_back(): lax.all_to_all(results, 'expert', split_axis=0, concat_axis=0, tiled=True)]
    pallas_call x0 -> x1, Pallas kernels: none -> 107 us  [kernel_device(): pl.pallas_call(functools.partial(kernel, n), out_shape=(jax.ShapeDtypeStr...]
    all_to_all x8 -> x0, starting transfers between devices: 54.5 us -> none  [the longest x4 34.9 us: send_back(): lax.all_to_all(results, 'expert', split_axis=0, concat_axis=0, tiled=True)]
    dot_general x12 -> x0, matrix products: 37.4 us -> none  [the longest x4 25.7 us: per_device(): jnp.dot(flat_rows, weights, preferred_element_type=jnp.float32)]
    ppermute x4 -> x0, waiting for transfers between devices: 37.4 us -> none  [swapped(): return lax.ppermute(value, axis, pairs)]
    ppermute x4 -> x0, starting transfers between devices: 5.86 us -> none  [swapped(): return lax.ppermute(value, axis, pairs)]
    unnamed x7 -> x4, local copies, waits for them, and re-layouts: 0.89 us -> 6.07 us
    another operation x3 -> x0, other arithmetic: 3.18 us -> none  [the longest x2 2.91 us: per_device(): return (jnp.stack(mixed_all), jnp.stack(swapped_all))]
  transfers between devices with their start and end apart: 12 -> 0, of which waited for: 10 -> 0; matrix products, arithmetic and copies ran while one was open for 15% -> 0% of each run, Pallas kernels for 0% -> 0%
where the time goes in v1:
time: 119 us; the launch traced here: 118 us
  Pallas kernels  107 us (90%)
  local copies, waits for them, and re-layouts  7.5 us (6%)
  other arithmetic  3.38 us (3%)
    pallas_call x1, Pallas kernels, kernel_device(): pl.pallas_call(functools.partial(kernel, n), out_shape=(jax.ShapeDtypeStr...  107 us
    unnamed x4, local copies, waits for them, and re-layouts  6.07 us

profile of v1, /device:TPU:0, one launch (start us, length us, event | category | flops | bytes accessed | tf_op | source)
XLA Modules:
  0.0 118.1 jit_solution(552630643462954113)
XLA Ops:
  0.6 1.3 %copy.20.pair_ref = s32[4,1]{1,0:T(4,128)} copy(s32[4,1]{0,1:T(1,128)} %param.11) | data formatting | bytes 32 | tf_op args[5]
  1.9 0.7 fusion
  2.7 0.7 multiply_divide_fusion
  3.4 0.1 copy.17
  3.5 0.7 reshape.17
  4.2 0.8 copy.16
  5.0 1.9 %select_reduce_fusion = s32[4,16,8]{2,1,0:T(8,128)S(1)} fusion(s32[16]{0:T(128)} %param.10, s32[4,16,8]{2,1,0:T(8,128)S(1)} %copy.16), kind=kLoop, calls=%fused_computation | loop fusion | flops 24064 | bytes 4160 | tf_op jit(solution)/shard_map/reduce_sum | solution.py:321
  6.9 0.7 reshape.16
  7.5 106.5 %shard_map.77 = (bf16[4,16,3584]{2,1,0:T(8,128)(2,1)}, bf16[4,1,32,3584]{3,2,1,0:T(8,128)(2,1)}) custom-call(bf16[4,128,1024]{2,1,0:T(8,128)(2,1)} %bitcast.5, bf16[1024,3584]{1,0:T(8,128)(2,1)} %bitcast.4, s32[4,1,128]{2,1,0:T(1,128)} %bitcast.7, f32[4,1,128]{2,1,0:T(1,128)} %bitcast.6, s32[4,1]{1,0:T(4,128)} %copy.20.pair_ref), custom_call_target="tpu_custom_call" | custom-call | tf_op jit(solution)/shard_map/pallas_call | solution.py:329
  114.1 1.8 %copy.23 = bf16[4,16,3584]{2,1,0:T(8,128)(2,1)} copy(bf16[4,16,3584]{2,1,0:T(8,128)(2,1)} %get-tuple-element.4) | data formatting | bytes 917504
  115.9 2.2 %copy.24 = bf16[4,1,32,3584]{3,2,1,0:T(8,128)(2,1)} copy(bf16[4,1,32,3584]{3,2,1,0:T(8,128)(2,1)} %get-tuple-element.5) | data formatting | bytes 1835008

commit v2 on v1

--- a/solution.py
+++ b/solution.py
@@ -9,6 +9,10 @@
 MESH = pl.DeviceIdType.MESH
 NSLICE = 32
 VMEM_BYTES = 60 * 2**20
+PARTS = 2
+TILES = 7
+DIRECT = 2
+AHEAD = 4
 
 
 ROUTE_SCALE = 2.5
@@ -81,17 +85,18 @@
 
 
 def kernel(
-    n, hidden_hbm, weight_hbm, owners_ref, gating_ref, pair_ref, mixed_ref, swapped_ref,
+    n, hidden_hbm, weight_hbm, logits_ref, routes_ref, placement_ref, pair_ref, mixed_ref, swapped_ref,
     hid, weights, outbox, inbox, acc, core_out, core_in, x_out, x_in,
     up_out, up_in, down_out, down_in, swap_out,
-    local_sem, hid_send, hid_recv, core_sem, x_sem, up_sem, down_sem, swap_sem,
+    local_sem, hid_send, hid_recv, core_sem, x_sem, up_sem, down_sem, plane_sem, swap_sem,
 ):
     steps = hid.shape[0]
     rows = hid.shape[1]
     tok = inbox.shape[2]
     top = rows // tok
-    width = weights.shape[1]
-    tile = 512
+    width = acc.shape[3]
+    parts = weights.shape[1] // width
+    tile = width // TILES
     planes = n // 4
     me = lax.axis_index("expert")
     c = lax.rem(me, 2)
@@ -107,7 +112,6 @@
     for s in range(steps):
         local(s).start()
     weight_copy.start()
-
     barrier = pltpu.get_barrier_semaphore()
 
     @pl.loop(1, n)
@@ -116,8 +120,6 @@
             barrier, inc=1, device_id={"expert": lax.rem(me + j, n)}, device_id_type=MESH
         )
 
-    pl.semaphore_wait(barrier, n - 1)
-
     def remote(src, dst, send, recv, target):
         return pltpu.make_async_remote_copy(
             src_ref=src, dst_ref=dst, send_sem=send, recv_sem=recv,
@@ -135,23 +137,51 @@
             hid_recv.at[s, source], source,
         )
 
+    f32 = jnp.float32
+    token = lax.broadcasted_iota(jnp.int32, (tok, rows), 0)
+    choice = lax.broadcasted_iota(jnp.int32, (tok, rows), 1)
+    spread = jnp.where(choice // top == token, 1.0, 0.0)
+    kth = lax.broadcasted_iota(jnp.int32, (top, rows), 0)
+    of_kth = lax.rem(lax.broadcasted_iota(jnp.int32, (top, rows), 1), top) == kth
+
+    def in_row(values):
+        wide = jnp.dot(
+            values, spread, precision=lax.Precision.HIGHEST, preferred_element_type=f32
+        )
+        return jnp.sum(jnp.where(of_kth, wide, 0.0), axis=0, keepdims=True)
+
     slot = lax.broadcasted_iota(jnp.int32, (n * tok, rows), 0)
-    choice = lax.broadcasted_iota(jnp.int32, (n * tok, rows), 1)
-    same_token = lax.rem(slot, tok) == choice // top
-    target_of = slot // tok
-    for s in range(steps):
-        picked = same_token & (owners_ref[s] == target_of)
-        scale = jnp.sum(jnp.where(picked, gating_ref[s], 0.0), axis=1, keepdims=True)
+    column = lax.broadcasted_iota(jnp.int32, (n * tok, rows), 1)
+    same_token = lax.rem(slot, tok) == column // top
+    target_of = (slot // tok).astype(f32)
+
+    def prepare(s):
+        scores = jax.nn.sigmoid(logits_ref[s])
+        gating = in_row(ROUTE_SCALE * scores / jnp.sum(scores, axis=0, keepdims=True))
+        routes = routes_ref[s]
+        owners = jnp.zeros((top, tok), jnp.int32)
+        for e in range(n):
+            owners = jnp.where(routes == e, placement_ref[e], owners)
+        picked = same_token & (in_row(owners.astype(f32)) == target_of)
+        scale = jnp.sum(jnp.where(picked, gating, 0.0), axis=1, keepdims=True)
         chosen = jnp.where(picked, 1.0, 0.0).astype(jnp.bfloat16)
         local(s).wait()
-        dense = jnp.dot(chosen, hid[s], preferred_element_type=jnp.float32) * scale
+        dense = jnp.dot(chosen, hid[s], preferred_element_type=f32) * scale
         outbox[s] = dense.astype(jnp.bfloat16).reshape(n, tok, dense.shape[1])
-
+        inbox[s, me] = outbox[s, me]
+
+    def send_hidden(s):
         @pl.loop(1, n)
         def _(j):
             hidden_to(s, lax.rem(me + j, n)).start()
 
-        inbox[s, me] = outbox[s, me]
+    prepare(0)
+    pl.semaphore_wait(barrier, n - 1)
+    send_hidden(0)
+    for s in range(1, steps):
+        prepare(s)
+        if s < AHEAD:
+            send_hidden(s)
 
     weight_copy.wait()
     levels = n.bit_length() - 1
@@ -159,10 +189,10 @@
     row = lax.broadcasted_iota(jnp.int32, (slice_rows, weights.shape[0]), 0)
     unit = lax.broadcasted_iota(jnp.int32, (slice_rows, weights.shape[0]), 1)
     handed = jnp.concatenate(
-        [jnp.where(unit == row + pair_ref[s, 0] * slice_rows, 1.0, 0.0) for s in range(steps)]
+        [jnp.where(unit == row + pair_ref[0, s] * slice_rows, 1.0, 0.0) for s in range(steps)]
     ).astype(jnp.bfloat16)
 
-    @pl.loop(0, width // tile)
+    @pl.loop(0, parts * TILES)
     def _(j):
         columns = pl.ds(pl.multiple_of(j * tile, tile), tile)
         block = jnp.dot(handed, weights[:, columns], preferred_element_type=jnp.float32)
@@ -194,17 +224,21 @@
             down_out.at[s, part], down_in.at[s, part], down_sem.at[0, s], down_sem.at[1, s], me - 4
         )
 
+    def arrive(s):
+        @pl.loop(1, n)
+        def _(j):
+            hidden_from(s, lax.rem(me + j, n)).wait_recv()
+
     def product(s):
-        @pl.loop(1, n)
-        def _(j):
-            hidden_from(s, lax.rem(me + j, n)).wait_recv()
-
-        @pl.loop(0, width // tile)
+        base = s % parts * width
+
+        @pl.loop(0, TILES)
         def _(j):
             columns = pl.ds(pl.multiple_of(j * tile, tile), tile)
             block = jnp.dot(
-                inbox[s].reshape(n * tok, inbox.shape[3]), weights[:, columns],
-                preferred_element_type=jnp.float32,
+                inbox[s // parts].reshape(n * tok, inbox.shape[3]),
+                weights[:, pl.ds(pl.multiple_of(base + j * tile, tile), tile)],
+                preferred_element_type=f32,
             )
             acc[s, :, :, columns] = block.reshape(n, tok, tile)
 
@@ -262,36 +296,88 @@
 
             down_copy(s, hop).start()
 
+    def plane_to(s, p):
+        return remote(
+            up_out.at[s, p], up_in.at[s, z], plane_sem.at[0, s, p], plane_sem.at[1, s, z],
+            me + 4 * (p - z),
+        )
+
+    def plane_from(s, p):
+        return remote(
+            up_out.at[s, p], up_in.at[s, p], plane_sem.at[0, s, p], plane_sem.at[1, s, p],
+            me + 4 * (p - z),
+        )
+
+    def to_planes(s):
+        x_copy(s).wait_recv()
+
+        @pl.loop(1, planes)
+        def _(j):
+            p = lax.rem(z + j, planes)
+            up_out[s, p] = plane_sum(s, p).astype(jnp.bfloat16)
+            plane_to(s, p).start()
+
+    def finish_direct(s):
+        @pl.loop(1, planes)
+        def _(j):
+            plane_from(s, lax.rem(z + j, planes)).wait_recv()
+
+        total = plane_sum(s, z)
+        for j in range(1, planes):
+            total = total + up_in[s, lax.rem(z + j, planes)].astype(f32)
+        mixed_ref[s // parts, :, pl.ds(s % parts * width, width)] = total.astype(mixed_ref.dtype)
+
     def finish(s):
+        columns = pl.ds(s % parts * width, width)
+
+        def put(total):
+            mixed_ref[s // parts, :, columns] = total.astype(mixed_ref.dtype)
+
         @pl.when(z == planes - 1)
         def _():
             up_copy(s, planes - 2).wait_recv()
-            mixed_ref[s] = (plane_sum(s, z) + up_in[s, z].astype(jnp.float32)).astype(mixed_ref.dtype)
+            put(plane_sum(s, z) + up_in[s, z].astype(f32))
 
         @pl.when(z == 0)
         def _():
             down_copy(s, planes - 2).wait_recv()
-            mixed_ref[s] = (plane_sum(s, z) + down_in[s, z].astype(jnp.float32)).astype(mixed_ref.dtype)
+            put(plane_sum(s, z) + down_in[s, z].astype(f32))
 
         @pl.when((z > 0) & (z < planes - 1))
         def _():
-            total = plane_sum(s, z) + up_in[s, z].astype(jnp.float32) + down_in[s, z].astype(jnp.float32)
-            mixed_ref[s] = total.astype(mixed_ref.dtype)
+            put(plane_sum(s, z) + up_in[s, z].astype(f32) + down_in[s, z].astype(f32))
 
     hops = planes - 1
-    for i in range(steps + hops + 1):
-        if i < steps:
+    chunks = steps * parts
+    chained = chunks - DIRECT
+    last_arrival = chunks - parts
+    for s in range(steps):
+        if s % levels >= levels - 2:
+            swaps[s].start()
+    for i in range(chunks + hops + 1):
+        if i < chunks:
+            if i % parts == 0:
+                arrive(i // parts)
+                if i // parts + AHEAD < steps:
+                    send_hidden(i // parts + AHEAD)
             product(i)
-            swaps[i].start()
+            if i == last_arrival:
+                for s in range(steps):
+                    if s % levels < levels - 2:
+                        swaps[s].start()
         for hop in range(hops - 1, 0, -1):
-            if 0 <= i - 1 - hop < steps:
+            if 0 <= i - 1 - hop < chained:
                 along_z(i - 1 - hop, hop)
-        if i < steps:
+        if i < chunks:
             across_x(i)
-        if 0 <= i - 1 < steps:
+        if 0 <= i - 1 < chained:
             along_z(i - 1, 0)
-        if 0 <= i - 1 - hops < steps:
+        if chained <= i - 1 < chunks:
+            to_planes(i - 1)
+        if 0 <= i - 1 - hops < chained:
             finish(i - 1 - hops)
+    for s in range(chained, chunks):
+        finish_direct(s)
 
     for s in range(steps):
         @pl.loop(1, n)
@@ -299,8 +385,15 @@
             hidden_to(s, lax.rem(me + j, n)).wait_send()
 
         swaps[s].wait()
+    for s in range(chunks):
         core_copy(s).wait_send()
         x_copy(s).wait_send()
+        if s >= chained:
+            @pl.loop(1, planes)
+            def _(j):
+                plane_to(s, lax.rem(z + j, planes)).wait_send()
+
+            continue
         for hop in range(hops):
             @pl.when(z == hop)
             def _():
@@ -317,40 +410,39 @@
     weights = down_weight[0]
     width = weights.shape[1]
     slice_rows = weights.shape[0] // NSLICE
-    expert_ids = jnp.arange(n, dtype=jnp.int32)
-    owners = jnp.sum(jnp.where(routes[..., None] == expert_ids, placement, 0), axis=-1)
-    scores = jax.nn.sigmoid(logits)
-    gating = ROUTE_SCALE * scores / jnp.sum(scores, axis=-1, keepdims=True)
     planes = n // 4
     b16, f32 = jnp.bfloat16, jnp.float32
     dma = pltpu.SemaphoreType.DMA
     anywhere = pl.BlockSpec(memory_space=pl.ANY)
     vmem = pl.BlockSpec(memory_space=pltpu.VMEM)
+    smem = pl.BlockSpec(memory_space=pltpu.SMEM)
+    chunks, part = steps * PARTS, width // PARTS
     return pl.pallas_call(
         functools.partial(kernel, n),
         out_shape=(
             jax.ShapeDtypeStruct((steps, tok, width), b16),
             jax.ShapeDtypeStruct((steps, 1, slice_rows, width), b16),
         ),
-        in_specs=[anywhere, anywhere, vmem, vmem, pl.BlockSpec(memory_space=pltpu.SMEM)],
+        in_specs=[anywhere, anywhere, vmem, vmem, smem, smem],
         out_specs=(vmem, anywhere),
         scratch_shapes=[
             pltpu.VMEM((steps, tok * top, hidden_cols), b16),
             pltpu.VMEM(weights.shape, b16),
             pltpu.VMEM((steps, n, tok, hidden_cols), b16),
             pltpu.VMEM((steps, n, tok, hidden_cols), b16),
-            pltpu.VMEM((steps, n, tok, width), f32),
-            pltpu.VMEM((steps, n // 2, tok, width), b16),
-            pltpu.VMEM((steps, n // 2, tok, width), b16),
-            pltpu.VMEM((steps, planes, tok, width), b16),
-            pltpu.VMEM((steps, planes, tok, width), b16),
-            pltpu.VMEM((steps, planes, tok, width), b16),
-            pltpu.VMEM((steps, planes, tok, width), b16),
-            pltpu.VMEM((steps, planes, tok, width), b16),
-            pltpu.VMEM((steps, planes, tok, width), b16),
+            pltpu.VMEM((chunks, n, tok, part), f32),
+            pltpu.VMEM((chunks, n // 2, tok, part), b16),
+            pltpu.VMEM((chunks, n // 2, tok, part), b16),
+            pltpu.VMEM((chunks, planes, tok, part), b16),
+            pltpu.VMEM((chunks, planes, tok, part), b16),
+            pltpu.VMEM((chunks, planes, tok, part), b16),
+            pltpu.VMEM((chunks, planes, tok, part), b16),
+            pltpu.VMEM((chunks, planes, tok, part), b16),
+            pltpu.VMEM((chunks, planes, tok, part), b16),
             pltpu.VMEM((steps, slice_rows, width), b16),
-            dma((steps + 1,)), dma((steps, n)), dma((steps, n)), dma((2, steps)), dma((2, steps)),
-            dma((2, steps)), dma((2, steps)), dma((2, steps)),
+            dma((steps + 1,)), dma((steps, n)), dma((steps, n)), dma((2, chunks)), dma((2, chunks)),
+            dma((2, chunks)), dma((2, chunks)), dma((2, chunks, planes)),
+            dma((2, steps)),
         ],
         compiler_params=pltpu.CompilerParams(
             collective_id=0, has_side_effects=True, vmem_limit_bytes=VMEM_BYTES
@@ -358,9 +450,10 @@
     )(
         hidden.reshape(steps, tok * top, hidden_cols),
         weights,
-        owners.reshape(steps, 1, tok * top),
-        gating.reshape(steps, 1, tok * top),
-        pair_slice,
+        logits.transpose(0, 2, 1),
+        routes.transpose(0, 2, 1),
+        placement,
+        pair_slice.T,
     )
 
 
@@ -371,7 +464,7 @@
     capacity = min(tok, 2 * ((tok * top + n - 1) // n))
     held = n * tok * width * steps * 11
     fits = n % 8 == 0 and capacity == tok and lax.axis_size("sub") == 1 and held < VMEM_BYTES
-    body = kernel_device if fits and width % 512 == 0 else plain_device
+    body = kernel_device if fits and width % (128 * PARTS * TILES) == 0 else plain_device
     return body(hidden, down_weight, logits, routes, placement, pair_slice)
 
 

time: 119 us -> 104 us (0.87)
  Pallas kernels: 107 us -> 99.1 us
  local copies, waits for them, and re-layouts: 7.5 us -> 3.98 us
  other arithmetic: 3.38 us -> 0 us
    pallas_call x1, Pallas kernels: 107 us -> 99.1 us  [kernel_device(): pl.pallas_call(functools.partial(kernel, n), out_shape=(jax.ShapeDtypeStr...]
    reduce_sum x2 -> x0, other arithmetic: 2.64 us -> none  [the longest x1 1.9 us: kernel_device(): jnp.sum(jnp.where(routes[..., None] == expert_ids, placement, 0), axis=-1)]
    unnamed x4 -> x2, local copies, waits for them, and re-layouts: 6.07 us -> 3.98 us
    reshape x2 -> x0, local copies, waits for them, and re-layouts: 1.35 us -> none  [the longest x1 0.68 us: kernel_device(): gating.reshape(steps, 1, tok * top)]
where the time goes in v2:
time: 104 us
  Pallas kernels  99.1 us (95%)
  local copies, waits for them, and re-layouts  3.98 us (4%)
    pallas_call x1, Pallas kernels, kernel_device(): pl.pallas_call(functools.partial(kernel, n), out_shape=(jax.ShapeDtypeStr...  99.1 us
    unnamed x2, local copies, waits for them, and re-layouts  3.98 us

profile of v2, /device:TPU:0, one launch (start us, length us, event | category | flops | bytes accessed | tf_op | source)
XLA Modules:
  0.0 103.7 jit_solution(3417848395281904471)
XLA Ops:
  0.6 99.1 %shard_map.77 = (bf16[4,16,3584]{2,1,0:T(8,128)(2,1)}, bf16[4,1,32,3584]{3,2,1,0:T(8,128)(2,1)}) custom-call(bf16[4,128,1024]{2,1,0:T(8,128)(2,1)} %bitcast.6, bf16[1024,3584]{1,0:T(8,128)(2,1)} %bitcast.5, f32[4,8,16]{2,1,0:T(8,128)} %bitcast.7, s32[4,8,16]{2,1,0:T(8,128)} %bitcast.8, s32[16]{0:T(128)} %placement_ref.1, s32[1,4]{1,0:T(1,128)} %bitcast.9), custom_call_target="tpu_custom_call" | custom-call | tf_op jit(solution)/shard_map/pallas_call | solution.py:420
  99.7 1.8 %copy.10 = bf16[4,16,3584]{2,1,0:T(8,128)(2,1)} copy(bf16[4,16,3584]{2,1,0:T(8,128)(2,1)} %get-tuple-element.4) | data formatting | bytes 917504
  101.5 2.2 %copy.11 = bf16[4,1,32,3584]{3,2,1,0:T(8,128)(2,1)} copy(bf16[4,1,32,3584]{3,2,1,0:T(8,128)(2,1)} %get-tuple-element.5) | data formatting | bytes 1835008

commit v3 on v2

--- a/solution.py
+++ b/solution.py
@@ -12,7 +12,7 @@
 PARTS = 2
 TILES = 7
 DIRECT = 2
-AHEAD = 4
+AHEAD = 1
 
 
 ROUTE_SCALE = 2.5

time: 104 us -> 107 us (1.029)
  Pallas kernels: 99.1 us -> 102 us
    pallas_call x1, Pallas kernels: 99.1 us -> 102 us  [kernel_device(): pl.pallas_call(functools.partial(kernel, n), out_shape=(jax.ShapeDtypeStr...]
where the time goes in v3:
time: 107 us
  Pallas kernels  102 us (95%)
  local copies, waits for them, and re-layouts  3.98 us (4%)
    pallas_call x1, Pallas kernels, kernel_device(): pl.pallas_call(functools.partial(kernel, n), out_shape=(jax.ShapeDtypeStr...  102 us
    unnamed x2, local copies, waits for them, and re-layouts  3.98 us

profile of v3, /device:TPU:0, one launch (start us, length us, event | category | flops | bytes accessed | tf_op | source)
XLA Modules:
  0.0 106.8 jit_solution(2755844975307511456)
XLA Ops:
  0.6 102.2 %shard_map.77 = (bf16[4,16,3584]{2,1,0:T(8,128)(2,1)}, bf16[4,1,32,3584]{3,2,1,0:T(8,128)(2,1)}) custom-call(bf16[4,128,1024]{2,1,0:T(8,128)(2,1)} %bitcast.6, bf16[1024,3584]{1,0:T(8,128)(2,1)} %bitcast.5, f32[4,8,16]{2,1,0:T(8,128)} %bitcast.7, s32[4,8,16]{2,1,0:T(8,128)} %bitcast.8, s32[16]{0:T(128)} %placement_ref.1, s32[1,4]{1,0:T(1,128)} %bitcast.9), custom_call_target="tpu_custom_call" | custom-call | tf_op jit(solution)/shard_map/pallas_call | solution.py:420
  102.8 1.8 %copy.10 = bf16[4,16,3584]{2,1,0:T(8,128)(2,1)} copy(bf16[4,16,3584]{2,1,0:T(8,128)(2,1)} %get-tuple-element.4) | data formatting | bytes 917504
  104.7 2.2 %copy.11 = bf16[4,1,32,3584]{3,2,1,0:T(8,128)(2,1)} copy(bf16[4,1,32,3584]{3,2,1,0:T(8,128)(2,1)} %get-tuple-element.5) | data formatting | bytes 1835008
